TPU v7x, 256 devices: a whole 4x4x8 slice. The times are simulated.
256 devices in a mesh: dp: 8 (over x, core), seq: 32 (over z, y).
Axes of the slice: x: 4, y: 4, z: 8, core: 2. Of those that a mesh axis runs over, the one named last changes fastest.
Arguments:
- x_rows: bfloat16 [8, 2048, 4096], P('dp', 'seq'), may hold values from -6 to 6
- router_weight: float32 [4096], replicated, may hold values from -0.09375 to 0.09375
- query_rows: bfloat16 [8, 2048, 4096], P('dp', 'seq'), may hold values from -8 to 8
- key_rows: bfloat16 [8, 2048, 4096], P('dp', 'seq'), may hold values from -8 to 8
- value_rows: bfloat16 [8, 2048, 4096], P('dp', 'seq'), may hold values from -6 to 6
- cotangent: bfloat16 [8, 2048, 4096], P('dp', 'seq'), may hold values from -6 to 6
- picked: int32 [8, 2048], P('dp', 'seq'), may hold values from -1 to 511, as said below
- dest_owner: int32 [8, 2048], P('dp', 'seq'), may hold values from -1 to 31, as said below
- dest_slot: int32 [8, 2048], P('dp', 'seq'), may hold values from -1 to 31, as said below
Outputs:
- blended: bfloat16 [8, 2048, 4096], P('dp', 'seq')
- grad_queries: bfloat16 [8, 2048, 4096], P('dp', 'seq')
- grad_keys: bfloat16 [8, 2048, 4096], P('dp', 'seq')
- grad_values: bfloat16 [8, 2048, 4096], P('dp', 'seq')
- logit_grad: float32 [8, 2048], P('dp', 'seq')
- router_grad: float32 [4096], replicated
Inputs may be any that keep to these rules, and one draw needn't show every extreme that they name: `picked`: in each shard the live slots come first and hold distinct token indices in increasing order; a shard has at most 64 live slots and in every sequence some shard has exactly 64; the live slots of a sequence number 1024; empty slots hold -1. Over a sequence's live slots the pairs (dest_owner, dest_slot) name each of the 32 x 32 places exactly once; no shard sends more than 2 rows to one owner, and some shard sends exactly 2; -1 at empty slots. `dest_slot`: see dest_owner; -1 at empty slots.
All inputs are finite; a program needn't handle non-finite values.
Results may differ from a plain program's by a relative error of at most 0.017.
Values may be sent and summed in bfloat16 or wider, within the bound.
A program may use at most 64 MiB of HBM per device.

v0:
```python
import functools

import jax
import jax.numpy as jnp
from jax import lax
from jax.experimental import pallas as pl
from jax.experimental.pallas import tpu as pltpu
from jax.sharding import PartitionSpec as P

HEAD_DIM = 128
MESH = pl.DeviceIdType.MESH
NEG = -1e30
LOG2E = 1.4426950408889634


def kernel(
    n_seq,
    n_dp,
    block,
    tile,
    x_hbm,
    w_hbm,
    q_hbm,
    k_hbm,
    v_hbm,
    c_hbm,
    picked_hbm,
    blend_out,
    dq_out,
    dk_out,
    dv_out,
    lg_ref,
    rg_ref,
    x_ref,
    c_ref,
    w_ref,
    picked_ref,
    gs_ref,
    count_ref,
    counts,
    bias_ref,
    qs,
    ks,
    vs,
    gs,
    e_ref,
    o_ref,
    inv_ref,
    at_ref,
    dq_ref,
    dk_ref,
    dv_ref,
    gt_ref,
    qt_ref,
    home_ref,
    part_ref,
    part_in,
    dp_in,
    full_ref,
    in_send,
    in_recv,
    out_send,
    out_recv,
    sum_send,
    sum_recv,
    local_sem,
):
    cap = x_ref.shape[0]
    width = x_ref.shape[1]
    total = n_seq * cap
    me = lax.axis_index("seq")
    dp = lax.axis_index("dp")
    f32 = jnp.float32
    bf16 = jnp.bfloat16
    n_z, n_y = n_seq // 4, 4

    def peer_of(n):
        t = lax.rem(n, n_z)
        dz = lax.div(t + 1, 2) * (2 * lax.rem(t, 2) - 1) + n_z
        dy = lax.div(n, n_z)
        z = lax.rem(lax.div(me, n_y) + dz, n_z)
        y = lax.rem(lax.rem(me, n_y) + dy, n_y)
        return z * n_y + y

    def cols(p):
        return pl.ds(pl.multiple_of(p * HEAD_DIM, HEAD_DIM), HEAD_DIM)

    def rows(p):
        return pl.ds(pl.multiple_of(p * cap, cap), cap)

    load_x = pltpu.make_async_copy(x_hbm.at[0], x_ref, local_sem.at[0])
    load_c = pltpu.make_async_copy(c_hbm.at[0], c_ref, local_sem.at[1])
    load_w = pltpu.make_async_copy(w_hbm, w_ref, local_sem.at[2])
    load_picked = pltpu.make_async_copy(picked_hbm, picked_ref, local_sem.at[3])
    load_picked.start()
    load_w.start()
    load_x.start()
    load_c.start()

    barrier = pltpu.get_barrier_semaphore()

    @pl.loop(1, n_seq)
    def _(n):
        pl.semaphore_signal(barrier, inc=1, device_id={"seq": peer_of(n)}, device_id_type=MESH)

    @pl.loop(1, n_dp)
    def _(n):
        pl.semaphore_signal(
            barrier, inc=1, device_id={"dp": lax.rem(dp + n, n_dp)}, device_id_type=MESH
        )

    load_picked.wait()
    live_row = (picked_ref[...] >= 0).astype(f32)
    count = jnp.sum(live_row, axis=1, keepdims=True)
    count_ref[0] = jnp.broadcast_to(count, (1, HEAD_DIM))
    live = lax.broadcasted_iota(jnp.int32, (cap, 1), 0).astype(f32) < count
    pl.semaphore_wait(barrier, n_seq + n_dp - 2)

    def spread(src_of, dst, send, recv, own):
        @pl.loop(1, n_seq)
        def _(n):
            p = peer_of(n_seq - n)
            pltpu.make_async_remote_copy(
                src_ref=src_of(p),
                dst_ref=dst,
                send_sem=send,
                recv_sem=recv,
                device_id={"seq": p},
                device_id_type=MESH,
            ).start()

        pltpu.make_async_copy(src_of(me), dst, own).start()

    for a, (src, dst) in enumerate(((k_hbm, ks), (q_hbm, qs), (v_hbm, vs))):
        spread(
            lambda p, src=src: src.at[0, :, cols(p)],
            dst.at[rows(me), pl.ds(0, HEAD_DIM)],
            in_send.at[a],
            in_recv.at[a],
            in_recv.at[a],
        )
        if a == 0:
            spread(
                lambda p: count_ref,
                counts.at[pl.ds(me, 1)],
                in_send.at[4],
                in_recv.at[4],
                in_recv.at[4],
            )

    load_x.wait()
    load_w.wait()
    logit = jnp.sum(x_ref[...].astype(f32) * w_ref[...], axis=1, keepdims=True)
    rate = jax.nn.sigmoid(logit)
    load_c.wait()
    scaled = (rate * c_ref[...].astype(f32)).astype(bf16)
    gs_ref[...] = jnp.where(live, scaled.astype(f32), 0.0).astype(bf16)
    spread(
        lambda p: gs_ref.at[:, cols(p)], gs.at[rows(me)], in_send.at[3], in_recv.at[3], in_recv.at[3]
    )

    vs[:, HEAD_DIM:] = jnp.ones((total, HEAD_DIM), bf16)

    pltpu.make_async_copy(counts, counts, in_recv.at[4]).wait()
    lane = lax.broadcasted_iota(jnp.int32, (1, HEAD_DIM), 1).astype(f32)
    for t in range(total // HEAD_DIM):
        bound = jnp.where(lane < cap, counts[2 * t], counts[2 * t + 1] + cap)
        bias_ref[:, t * HEAD_DIM : (t + 1) * HEAD_DIM] = jnp.where(lane < bound, 0.0, NEG)

    def wait_all(ref, sem):
        pltpu.make_async_copy(ref, ref, sem).wait()

    scale = HEAD_DIM ** (-0.5)
    factor = scale * LOG2E
    n_blocks = total // block
    n_tiles = block // tile
    nt = (((1,), (1,)), ((), ()))

    def dot(a, b):
        return jnp.dot(a, b, preferred_element_type=f32)

    def dot_t(a, b):
        return lax.dot_general(a, b, nt, preferred_element_type=f32)

    wait_all(ks, in_recv.at[0])
    wait_all(qs, in_recv.at[1])

    for i in range(n_blocks):
        wide = (i + 1) * block

        @pl.loop(0, n_tiles)
        def _(r, i=i, wide=wide):
            here = pl.ds(pl.multiple_of(i * block + r * tile, tile), tile)
            s = dot_t(qs[here, :], ks[:wide, :]) * factor + bias_ref[:, :wide]
            diag = s[:, i * block :]
            row = lax.broadcasted_iota(jnp.int32, diag.shape, 0) + r * tile
            col = lax.broadcasted_iota(jnp.int32, diag.shape, 1)
            diag = jnp.where(col <= row, diag, NEG)
            top = jnp.max(diag, axis=1, keepdims=True)
            if i > 0:
                off = s[:, : i * block]
                top = jnp.maximum(top, jnp.max(off, axis=1, keepdims=True))
                e_ref[here, : i * block] = jnp.exp2(off - top).astype(bf16)
            e_ref[here, i * block : wide] = jnp.exp2(diag - top).astype(bf16)

    wait_all(vs.at[:, pl.ds(0, HEAD_DIM)], in_recv.at[2])

    for i in range(n_blocks):
        wide = (i + 1) * block

        @pl.loop(0, n_tiles)
        def _(r, i=i, wide=wide):
            here = pl.ds(pl.multiple_of(i * block + r * tile, tile), tile)
            both = dot(e_ref[here, :wide], vs[:wide, :])
            inv = 1.0 / both[:, HEAD_DIM:]
            out = both[:, :HEAD_DIM] * inv
            inv_ref[here, :] = inv
            o_ref[here, :] = out
            at_ref[here, :] = out.astype(bf16)

    def give_back(src, dst, send, recv, first=0, last=n_seq):
        @pl.loop(max(first, 1), last)
        def _(n):
            p = peer_of(n_seq - n)
            pltpu.make_async_remote_copy(
                src_ref=src.at[rows(p), :],
                dst_ref=dst.at[:, cols(me)],
                send_sem=send,
                recv_sem=recv,
                device_id={"seq": p},
                device_id_type=MESH,
            ).start()

        if first == 0:
            pltpu.make_async_copy(src.at[rows(me), :], dst.at[:, cols(me)], recv).start()

    give_back(at_ref, home_ref, out_send.at[0], out_recv.at[0])

    wait_all(gs, in_recv.at[3])

    @pl.loop(0, total // HEAD_DIM)
    def _(t):
        here = pl.ds(pl.multiple_of(t * HEAD_DIM, HEAD_DIM), HEAD_DIM)
        inv = inv_ref[here, :]
        gt_ref[:, here] = (gs[here, :].astype(f32) * inv).T.astype(bf16)
        qt_ref[:, here] = (qs[here, :].astype(f32) * (inv * scale)).T.astype(bf16)

    for j in range(n_blocks):
        lo = j * block
        res = dot(gt_ref[:, lo:], e_ref[lo:, lo : lo + block])
        dv_ref[lo : lo + block, :] = res.T.astype(bf16)
    give_back(dv_ref, dv_out.at[0], out_send.at[1], out_recv.at[1])

    for i in range(n_blocks):
        wide = (i + 1) * block

        @pl.loop(0, n_tiles)
        def _(r, i=i, wide=wide):
            here = pl.ds(pl.multiple_of(i * block + r * tile, tile), tile)
            g = gs[here, :]
            mean = jnp.sum(g.astype(f32) * o_ref[here, :], axis=1, keepdims=True)
            dprob = dot_t(g, vs[:wide, :HEAD_DIM])
            ds = (e_ref[here, :wide].astype(f32) * (dprob - mean)).astype(bf16)
            e_ref[here, :wide] = ds
            dq = dot(ds, ks[:wide, :]) * (inv_ref[here, :] * scale)
            dq_ref[here, :] = dq.astype(bf16)

    wait_all(home_ref, out_recv.at[0])
    attn = home_ref[...].astype(f32)
    blend_out[0] = jnp.where(live, rate * attn, 0.0).astype(bf16)
    dotted = jnp.sum(c_ref[...].astype(f32) * attn, axis=1, keepdims=True)
    lg = jnp.where(live, dotted * rate * (1.0 - rate), 0.0)
    eye = lax.broadcasted_iota(jnp.int32, (cap, cap), 0) == lax.broadcasted_iota(
        jnp.int32, (cap, cap), 1
    )
    lg_ref[...] = jnp.sum(jnp.where(eye, lg, 0.0), axis=0, keepdims=True)
    part = jnp.sum(lg * x_ref[...].astype(f32), axis=0, keepdims=True)
    for p in range(n_seq):
        part_ref[p] = part[:, p * HEAD_DIM : (p + 1) * HEAD_DIM]

    spread(
        lambda p: part_ref.at[pl.ds(p, 1)],
        part_in.at[pl.ds(me, 1)],
        sum_send.at[0],
        sum_recv.at[0],
        sum_recv.at[0],
    )
    give_back(dq_ref, dq_out.at[0], out_send.at[2], out_recv.at[2])

    for j in range(n_blocks):
        lo = j * block
        res = dot(qt_ref[:, lo:], e_ref[lo:, lo : lo + block])
        dk_ref[lo : lo + block, :] = res.T.astype(bf16)
    wait_all(part_in, sum_recv.at[0])
    count_sum = jnp.sum(part_in[...], axis=0, keepdims=True)
    dp_in[pl.ds(dp, 1)] = count_sum

    @pl.loop(1, n_dp)
    def _(n):
        pltpu.make_async_remote_copy(
            src_ref=dp_in.at[pl.ds(dp, 1)],
            dst_ref=dp_in.at[pl.ds(dp, 1)],
            send_sem=sum_send.at[1],
            recv_sem=sum_recv.at[1],
            device_id={"dp": lax.rem(dp + n, n_dp)},
            device_id_type=MESH,
        ).start()

    give_back(dk_ref, dk_out.at[0], out_send.at[3], out_recv.at[3], 0, n_seq // 2)
    wait_all(dp_in.at[pl.ds(0, n_dp - 1)], sum_recv.at[1])
    full_ref[pl.ds(me, 1)] = jnp.sum(dp_in[...], axis=0, keepdims=True)

    @pl.loop(1, n_seq)
    def _(n):
        pltpu.make_async_remote_copy(
            src_ref=full_ref.at[pl.ds(me, 1)],
            dst_ref=full_ref.at[pl.ds(me, 1)],
            send_sem=sum_send.at[2],
            recv_sem=sum_recv.at[2],
            device_id={"seq": peer_of(n)},
            device_id_type=MESH,
        ).start()

    give_back(dk_ref, dk_out.at[0], out_send.at[3], out_recv.at[3], n_seq // 2, n_seq)

    wait_all(full_ref.at[pl.ds(0, n_seq - 1)], sum_recv.at[2])
    for p in range(n_seq):
        rg_ref[:, p * HEAD_DIM : (p + 1) * HEAD_DIM] = full_ref[p]

    sent = pl.ds(0, total - cap)
    most = pl.ds(0, n_seq - 1)
    for a in range(4):
        wait_all(ks.at[sent, :], in_send.at[a])
    wait_all(counts.at[most], in_send.at[4])
    wait_all(counts.at[most], sum_send.at[0])
    wait_all(dp_in.at[pl.ds(0, n_dp - 1)], sum_send.at[1])
    wait_all(counts.at[most], sum_send.at[2])
    for a in range(3):
        wait_all(ks.at[sent, :], out_send.at[a])
    wait_all(dv_out, out_recv.at[1])
    wait_all(dq_out, out_recv.at[2])
    wait_all(ks.at[sent, :], out_send.at[3])
    wait_all(dk_out, out_recv.at[3])


def write_out(n, *refs):
    sems = refs[2 * n]
    copies = [pltpu.make_async_copy(refs[a], refs[n + a], sems.at[a]) for a in range(n)]
    for copy in copies:
        copy.start()
    for copy in copies:
        copy.wait()


def body(x_rows, router_weight, query_rows, key_rows, value_rows, cotangent, picked):
    n_seq = lax.axis_size("seq")
    n_dp = lax.axis_size("dp")
    _, cap, width = x_rows.shape
    total = n_seq * cap
    block = min(512, total // 2)
    tile = 128
    f32 = jnp.float32
    bf16 = jnp.bfloat16
    anyspace = pl.BlockSpec(memory_space=pl.ANY)
    hbm = pl.BlockSpec(memory_space=pltpu.HBM)
    vmem = pl.BlockSpec(memory_space=pltpu.VMEM)
    big = pltpu.VMEM(x_rows.shape, bf16)
    head = pltpu.VMEM((total, HEAD_DIM), bf16)
    headf = pltpu.VMEM((total, HEAD_DIM), f32)
    own = pltpu.VMEM((cap, width), bf16)
    chunks = pltpu.VMEM((n_seq, 1, HEAD_DIM), f32)
    out = pl.pallas_call(
        functools.partial(kernel, n_seq, n_dp, block, tile),
        out_shape=(
            big,
            big,
            big,
            big,
            pltpu.VMEM((1, cap), f32),
            pltpu.VMEM((1, width), f32),
        ),
        in_specs=[hbm] * 7,
        out_specs=(vmem,) * 6,
        scratch_shapes=[
            own,
            own,
            pltpu.VMEM((1, width), f32),
            pltpu.VMEM((1, cap), jnp.int32),
            own,
            pltpu.VMEM((1, 1, HEAD_DIM), f32),
            chunks,
            pltpu.VMEM((1, total), f32),
            head,
            head,
            pltpu.VMEM((total, 2 * HEAD_DIM), bf16),
            head,
            pltpu.VMEM((total, total), bf16),
            headf,
            headf,
            head,
            head,
            head,
            head,
            pltpu.VMEM((HEAD_DIM, total), bf16),
            pltpu.VMEM((HEAD_DIM, total), bf16),
            own,
            chunks,
            chunks,
            pltpu.VMEM((n_dp, 1, HEAD_DIM), f32),
            chunks,
            pltpu.SemaphoreType.DMA((5,)),
            pltpu.SemaphoreType.DMA((5,)),
            pltpu.SemaphoreType.DMA((4,)),
            pltpu.SemaphoreType.DMA((4,)),
            pltpu.SemaphoreType.DMA((3,)),
            pltpu.SemaphoreType.DMA((3,)),
            pltpu.SemaphoreType.DMA((4,)),
        ],
        compiler_params=pltpu.CompilerParams(
            collective_id=0, has_side_effects=True, vmem_limit_bytes=48 * 1024 * 1024
        ),
    )(
        *(
            pltpu.with_memory_space_constraint(a, pltpu.HBM)
            for a in (
                x_rows,
                router_weight.reshape(1, width),
                query_rows,
                key_rows,
                value_rows,
                cotangent,
                picked,
            )
        )
    )
    blended, grad_q, grad_k, grad_v, logit_grad, router_grad = pl.pallas_call(
        functools.partial(write_out, len(out)),
        out_shape=tuple(pltpu.HBM(o.shape, o.dtype) for o in out),
        in_specs=[vmem] * len(out),
        out_specs=(hbm,) * len(out),
        scratch_shapes=[pltpu.SemaphoreType.DMA((len(out),))],
        compiler_params=pltpu.CompilerParams(vmem_limit_bytes=16 * 1024 * 1024),
    )(*out)
    return blended, grad_q, grad_k, grad_v, logit_grad, router_grad.reshape(width)


def solution(mesh):
    row3 = P("dp", "seq", None)
    row2 = P("dp", "seq")
    mapped = jax.shard_map(
        body,
        mesh=mesh,
        in_specs=(row3, P(), row3, row3, row3, row3, row2),
        out_specs=(row3, row3, row3, row3, row2, P()),
        check_vma=False,
    )

    def run(
        x_rows,
        router_weight,
        query_rows,
        key_rows,
        value_rows,
        cotangent,
        picked,
        dest_owner,
        dest_slot,
    ):
        return mapped(
            x_rows, router_weight, query_rows, key_rows, value_rows, cotangent, picked
        )

    return run
```

profile of v0, /device:TPU:1, one launch (start us, length us, event | category | flops | bytes accessed | tf_op | source)
XLA Modules:
  0.0 105.2 jit_solution(1951007813127378613)
XLA Ops:
  0.6 103.2 %shard_map.118 = (bf16[1,64,4096]{2,1,0:T(8,128)(2,1)S(1)}, bf16[1,64,4096]{2,1,0:T(8,128)(2,1)S(1)}, bf16[1,64,4096]{2,1,0:T(8,128)(2,1)S(1)}, bf16[1,64,4096]{...) custom-call(bf16[1,64,4096]{2,1,0:T(8,128)(2,1)} %x_hbm.1, f32[1,4096]{1,0:T(1,128)} %bitcast.2, ...), custom_call_target="tpu_custom_call" | custom-call | tf_op jit(solution)/shard_map/pallas_call | solution.py:372
  103.8 1.4 %shard_map.119 = (bf16[1,64,4096]{2,1,0:T(8,128)(2,1)}, bf16[1,64,4096]{2,1,0:T(8,128)(2,1)}, bf16[1,64,4096]{2,1,0:T(8,128)(2,1)}, bf16[1,64,4096]{2,1,0:T(8,12...) custom-call(bf16[1,64,4096]{2,1,0:T(8,128)(2,1)S(1)} %get-tuple-element.18.refs_0_, ...), custom_call_target="tpu_custom_call" | custom-call | tf_op jit(solution)/shard_map/pallas_call | solution.py:436
where the time goes:
time: 105 us
  Pallas kernels  105 us (100%)
    pallas_call x1, Pallas kernels, body(): pl.pallas_call(functools.partial(kernel, n_seq, n_dp, block, tile), out_s...  103 us

commit v1 on v0

--- a/solution.py
+++ b/solution.py
@@ -26,8 +26,7 @@
     c_hbm,
     picked_hbm,
     blend_out,
-    dq_out,
-    dk_out,
+    dqk_out,
     dv_out,
     lg_ref,
     rg_ref,
@@ -39,16 +38,15 @@
     count_ref,
     counts,
     bias_ref,
-    qs,
-    ks,
+    stage_ref,
+    kq,
     vs,
     gs,
     e_ref,
     o_ref,
     inv_ref,
     at_ref,
-    dq_ref,
-    dk_ref,
+    dqk_ref,
     dv_ref,
     gt_ref,
     qt_ref,
@@ -92,7 +90,11 @@
     load_c = pltpu.make_async_copy(c_hbm.at[0], c_ref, local_sem.at[1])
     load_w = pltpu.make_async_copy(w_hbm, w_ref, local_sem.at[2])
     load_picked = pltpu.make_async_copy(picked_hbm, picked_ref, local_sem.at[3])
+    load_k = pltpu.make_async_copy(k_hbm.at[0], stage_ref.at[0], local_sem.at[4])
+    load_q = pltpu.make_async_copy(q_hbm.at[0], stage_ref.at[1], local_sem.at[5])
     load_picked.start()
+    load_k.start()
+    load_q.start()
     load_w.start()
     load_x.start()
     load_c.start()
@@ -114,6 +116,8 @@
     count = jnp.sum(live_row, axis=1, keepdims=True)
     count_ref[0] = jnp.broadcast_to(count, (1, HEAD_DIM))
     live = lax.broadcasted_iota(jnp.int32, (cap, 1), 0).astype(f32) < count
+    load_k.wait()
+    load_q.wait()
     pl.semaphore_wait(barrier, n_seq + n_dp - 2)
 
     def spread(src_of, dst, send, recv, own):
@@ -131,22 +135,23 @@
 
         pltpu.make_async_copy(src_of(me), dst, own).start()
 
-    for a, (src, dst) in enumerate(((k_hbm, ks), (q_hbm, qs), (v_hbm, vs))):
-        spread(
-            lambda p, src=src: src.at[0, :, cols(p)],
-            dst.at[rows(me), pl.ds(0, HEAD_DIM)],
-            in_send.at[a],
-            in_recv.at[a],
-            in_recv.at[a],
-        )
-        if a == 0:
-            spread(
-                lambda p: count_ref,
-                counts.at[pl.ds(me, 1)],
-                in_send.at[4],
-                in_recv.at[4],
-                in_recv.at[4],
-            )
+    spread(
+        lambda p: stage_ref.at[:, :, cols(p)],
+        kq.at[:, rows(me), :],
+        in_send.at[0],
+        in_recv.at[0],
+        in_recv.at[0],
+    )
+    spread(
+        lambda p: count_ref, counts.at[pl.ds(me, 1)], in_send.at[4], in_recv.at[4], in_recv.at[4]
+    )
+    spread(
+        lambda p: v_hbm.at[0, :, cols(p)],
+        vs.at[rows(me), pl.ds(0, HEAD_DIM)],
+        in_send.at[2],
+        in_recv.at[2],
+        in_recv.at[2],
+    )
 
     load_x.wait()
     load_w.wait()
@@ -182,8 +187,7 @@
     def dot_t(a, b):
         return lax.dot_general(a, b, nt, preferred_element_type=f32)
 
-    wait_all(ks, in_recv.at[0])
-    wait_all(qs, in_recv.at[1])
+    wait_all(kq, in_recv.at[0])
 
     for i in range(n_blocks):
         wide = (i + 1) * block
@@ -191,7 +195,7 @@
         @pl.loop(0, n_tiles)
         def _(r, i=i, wide=wide):
             here = pl.ds(pl.multiple_of(i * block + r * tile, tile), tile)
-            s = dot_t(qs[here, :], ks[:wide, :]) * factor + bias_ref[:, :wide]
+            s = dot_t(kq[1, here, :], kq[0, :wide, :]) * factor + bias_ref[:, :wide]
             diag = s[:, i * block :]
             row = lax.broadcasted_iota(jnp.int32, diag.shape, 0) + r * tile
             col = lax.broadcasted_iota(jnp.int32, diag.shape, 1)
@@ -219,12 +223,14 @@
             at_ref[here, :] = out.astype(bf16)
 
     def give_back(src, dst, send, recv, first=0, last=n_seq):
+        lead = (slice(None),) * (len(src.shape) - 2)
+
         @pl.loop(max(first, 1), last)
         def _(n):
             p = peer_of(n_seq - n)
             pltpu.make_async_remote_copy(
-                src_ref=src.at[rows(p), :],
-                dst_ref=dst.at[:, cols(me)],
+                src_ref=src.at[(*lead, rows(p), slice(None))],
+                dst_ref=dst.at[(*lead, slice(None), cols(me))],
                 send_sem=send,
                 recv_sem=recv,
                 device_id={"seq": p},
@@ -232,7 +238,11 @@
             ).start()
 
         if first == 0:
-            pltpu.make_async_copy(src.at[rows(me), :], dst.at[:, cols(me)], recv).start()
+            pltpu.make_async_copy(
+                src.at[(*lead, rows(me), slice(None))],
+                dst.at[(*lead, slice(None), cols(me))],
+                recv,
+            ).start()
 
     give_back(at_ref, home_ref, out_send.at[0], out_recv.at[0])
 
@@ -243,7 +253,7 @@
         here = pl.ds(pl.multiple_of(t * HEAD_DIM, HEAD_DIM), HEAD_DIM)
         inv = inv_ref[here, :]
         gt_ref[:, here] = (gs[here, :].astype(f32) * inv).T.astype(bf16)
-        qt_ref[:, here] = (qs[here, :].astype(f32) * (inv * scale)).T.astype(bf16)
+        qt_ref[:, here] = (kq[1, here, :].astype(f32) * (inv * scale)).T.astype(bf16)
 
     for j in range(n_blocks):
         lo = j * block
@@ -262,9 +272,13 @@
             dprob = dot_t(g, vs[:wide, :HEAD_DIM])
             ds = (e_ref[here, :wide].astype(f32) * (dprob - mean)).astype(bf16)
             e_ref[here, :wide] = ds
-            dq = dot(ds, ks[:wide, :]) * (inv_ref[here, :] * scale)
-            dq_ref[here, :] = dq.astype(bf16)
-
+            dq = dot(ds, kq[0, :wide, :]) * (inv_ref[here, :] * scale)
+            dqk_ref[0, here, :] = dq.astype(bf16)
+
+    for j in range(n_blocks):
+        lo = j * block
+        res = dot(qt_ref[:, lo:], e_ref[lo:, lo : lo + block])
+        dqk_ref[1, lo : lo + block, :] = res.T.astype(bf16)
     wait_all(home_ref, out_recv.at[0])
     attn = home_ref[...].astype(f32)
     blend_out[0] = jnp.where(live, rate * attn, 0.0).astype(bf16)
@@ -285,12 +299,8 @@
         sum_recv.at[0],
         sum_recv.at[0],
     )
-    give_back(dq_ref, dq_out.at[0], out_send.at[2], out_recv.at[2])
-
-    for j in range(n_blocks):
-        lo = j * block
-        res = dot(qt_ref[:, lo:], e_ref[lo:, lo : lo + block])
-        dk_ref[lo : lo + block, :] = res.T.astype(bf16)
+    give_back(dqk_ref, dqk_out, out_send.at[2], out_recv.at[2], 0, n_seq // 3)
+
     wait_all(part_in, sum_recv.at[0])
     count_sum = jnp.sum(part_in[...], axis=0, keepdims=True)
     dp_in[pl.ds(dp, 1)] = count_sum
@@ -306,7 +316,7 @@
             device_id_type=MESH,
         ).start()
 
-    give_back(dk_ref, dk_out.at[0], out_send.at[3], out_recv.at[3], 0, n_seq // 2)
+    give_back(dqk_ref, dqk_out, out_send.at[2], out_recv.at[2], n_seq // 3, 2 * n_seq // 3)
     wait_all(dp_in.at[pl.ds(0, n_dp - 1)], sum_recv.at[1])
     full_ref[pl.ds(me, 1)] = jnp.sum(dp_in[...], axis=0, keepdims=True)
 
@@ -321,7 +331,7 @@
             device_id_type=MESH,
         ).start()
 
-    give_back(dk_ref, dk_out.at[0], out_send.at[3], out_recv.at[3], n_seq // 2, n_seq)
+    give_back(dqk_ref, dqk_out, out_send.at[2], out_recv.at[2], 2 * n_seq // 3, n_seq)
 
     wait_all(full_ref.at[pl.ds(0, n_seq - 1)], sum_recv.at[2])
     for p in range(n_seq):
@@ -329,23 +339,34 @@
 
     sent = pl.ds(0, total - cap)
     most = pl.ds(0, n_seq - 1)
-    for a in range(4):
-        wait_all(ks.at[sent, :], in_send.at[a])
+    wait_all(kq.at[:, sent, :], in_send.at[0])
+    wait_all(gs.at[sent, :], in_send.at[2])
+    wait_all(gs.at[sent, :], in_send.at[3])
     wait_all(counts.at[most], in_send.at[4])
     wait_all(counts.at[most], sum_send.at[0])
     wait_all(dp_in.at[pl.ds(0, n_dp - 1)], sum_send.at[1])
     wait_all(counts.at[most], sum_send.at[2])
-    for a in range(3):
-        wait_all(ks.at[sent, :], out_send.at[a])
+    wait_all(gs.at[sent, :], out_send.at[0])
+    wait_all(gs.at[sent, :], out_send.at[1])
     wait_all(dv_out, out_recv.at[1])
-    wait_all(dq_out, out_recv.at[2])
-    wait_all(ks.at[sent, :], out_send.at[3])
-    wait_all(dk_out, out_recv.at[3])
-
-
-def write_out(n, *refs):
-    sems = refs[2 * n]
-    copies = [pltpu.make_async_copy(refs[a], refs[n + a], sems.at[a]) for a in range(n)]
+    wait_all(kq.at[:, sent, :], out_send.at[2])
+    wait_all(dqk_out, out_recv.at[2])
+
+
+def write_out(blended, pair, grad_v, logit, router, o_b, o_q, o_k, o_v, o_l, o_r, sems):
+    copies = [
+        pltpu.make_async_copy(src, dst, sems.at[a])
+        for a, (src, dst) in enumerate(
+            (
+                (blended, o_b),
+                (pair.at[pl.ds(0, 1)], o_q),
+                (pair.at[pl.ds(1, 1)], o_k),
+                (grad_v, o_v),
+                (logit, o_l),
+                (router, o_r),
+            )
+        )
+    ]
     for copy in copies:
         copy.start()
     for copy in copies:
@@ -373,14 +394,13 @@
         functools.partial(kernel, n_seq, n_dp, block, tile),
         out_shape=(
             big,
-            big,
-            big,
+            pltpu.VMEM((2, cap, width), bf16),
             big,
             pltpu.VMEM((1, cap), f32),
             pltpu.VMEM((1, width), f32),
         ),
         in_specs=[hbm] * 7,
-        out_specs=(vmem,) * 6,
+        out_specs=(vmem,) * 5,
         scratch_shapes=[
             own,
             own,
@@ -390,16 +410,15 @@
             pltpu.VMEM((1, 1, HEAD_DIM), f32),
             chunks,
             pltpu.VMEM((1, total), f32),
-            head,
-            head,
+            pltpu.VMEM((2, cap, width), bf16),
+            pltpu.VMEM((2, total, HEAD_DIM), bf16),
             pltpu.VMEM((total, 2 * HEAD_DIM), bf16),
             head,
             pltpu.VMEM((total, total), bf16),
             headf,
             headf,
             head,
-            head,
-            head,
+            pltpu.VMEM((2, total, HEAD_DIM), bf16),
             head,
             pltpu.VMEM((HEAD_DIM, total), bf16),
             pltpu.VMEM((HEAD_DIM, total), bf16),
@@ -414,7 +433,7 @@
             pltpu.SemaphoreType.DMA((4,)),
             pltpu.SemaphoreType.DMA((3,)),
             pltpu.SemaphoreType.DMA((3,)),
-            pltpu.SemaphoreType.DMA((4,)),
+            pltpu.SemaphoreType.DMA((6,)),
         ],
         compiler_params=pltpu.CompilerParams(
             collective_id=0, has_side_effects=True, vmem_limit_bytes=48 * 1024 * 1024
@@ -434,11 +453,12 @@
         )
     )
     blended, grad_q, grad_k, grad_v, logit_grad, router_grad = pl.pallas_call(
-        functools.partial(write_out, len(out)),
-        out_shape=tuple(pltpu.HBM(o.shape, o.dtype) for o in out),
+        write_out,
+        out_shape=(pltpu.HBM(x_rows.shape, bf16),) * 4
+        + (pltpu.HBM((1, cap), f32), pltpu.HBM((1, width), f32)),
         in_specs=[vmem] * len(out),
-        out_specs=(hbm,) * len(out),
-        scratch_shapes=[pltpu.SemaphoreType.DMA((len(out),))],
+        out_specs=(hbm,) * 6,
+        scratch_shapes=[pltpu.SemaphoreType.DMA((6,))],
         compiler_params=pltpu.CompilerParams(vmem_limit_bytes=16 * 1024 * 1024),
     )(*out)
     return blended, grad_q, grad_k, grad_v, logit_grad, router_grad.reshape(width)

time: 105 us -> 105 us (level)
  no operation moved by 1% of the time
where the time goes in v1:
time: 105 us
  Pallas kernels  105 us (100%)
    pallas_call x1, Pallas kernels, body(): pl.pallas_call(functools.partial(kernel, n_seq, n_dp, block, tile), out_s...  103 us

profile of v1, /device:TPU:1, one launch (start us, length us, event | category | flops | bytes accessed | tf_op | source)
XLA Modules:
  0.0 105.3 jit_solution(4756166298269690432)
XLA Ops:
  0.6 103.3 %shard_map.118 = (bf16[1,64,4096]{2,1,0:T(8,128)(2,1)S(1)}, bf16[2,64,4096]{2,1,0:T(8,128)(2,1)S(1)}, bf16[1,64,4096]{2,1,0:T(8,128)(2,1)S(1)}, f32[1,64]{1,0:T(1,128)S(1)}, f32[1,4096]{1,0:T(1,128)S(1)}) custom-call(bf16[1,64,4096]{2,1,0:T(8,128)(2,1)} %x_hbm.1, f32[1,4096]{1,0:T(1,128)} %bitcast.2, bf16[1,64,4096]{2,1,0:T(8,128)(2,1)} %q_hbm.1, ...), custom_call_target="tpu_custom_call" | custom-call | tf_op jit(solution)/shard_map/pallas_call | solution.py:393
  103.9 1.4 %shard_map.119 = (bf16[1,64,4096]{2,1,0:T(8,128)(2,1)}, bf16[1,64,4096]{2,1,0:T(8,128)(2,1)}, bf16[1,64,4096]{2,1,0:T(8,128)(2,1)}, bf16[1,64,4096]{2,1,0:T(8,12...) custom-call(bf16[1,64,4096]{2,1,0:T(8,128)(2,1)S(1)} %get-tuple-element.17.blended, ...), custom_call_target="tpu_custom_call" | custom-call | tf_op jit(solution)/shard_map/pallas_call | solution.py:455
